TPU v7x, 256 devices: a whole 4x4x8 slice. The times are simulated.
256 devices in a mesh: dp: 16 (over z, core), mp: 16 (over x, y).
Axes of the slice: x: 4, y: 4, z: 8, core: 2. Of those that a mesh axis runs over, the one named last changes fastest.
Arguments:
- hidden_in: bfloat16 [64, 64, 7168], P('dp', None, 'mp'), may hold values from -6 to 6
- norm_gain: bfloat16 [7168], P('mp'), may hold values from 0.099609375 to 1.8984375
- w_query: bfloat16 [7168, 7168], P('dp', 'mp'), may hold values from -0.070868339 to 0.070868339
- w_key: bfloat16 [7168, 1024], P('dp', 'mp'), may hold values from -0.070868339 to 0.070868339
- w_value: bfloat16 [7168, 1024], P('dp', 'mp'), may hold values from -0.0625 to 0.0625
- w_out: bfloat16 [7168, 7168], P('mp', 'dp'), may hold values from -0.09375 to 0.09375
- key_cache: bfloat16 [64, 16, 1, 2048, 128], P('dp', 'mp'), may hold values from -52 to 52
- value_cache: bfloat16 [64, 16, 1, 2048, 128], P('dp', 'mp'), may hold values from -3 to 3
- cache_len: int32 [64], P('dp'), may hold values from 256 to 4096, as said below
- tree_parent: int32 [64, 64], P('dp'), may hold values from 0 to 62, as said below
- valid_nodes: int32 [64, 64], P('dp'), may hold values from 0 to 1, as said below
- accepted_path: int32 [64, 8], P('dp'), may hold values from 0 to 63, as said below
- slot_owner: int32 [64], replicated, may hold values from 0 to 63, each once
Outputs:
- layer_out: bfloat16 [64, 64, 7168], P('dp', None, 'mp')
- accepted_kv: bfloat16 [64, 8, 2, 1024], P('dp', None, None, 'mp')
Inputs may be any that keep to these rules, and one draw needn't show every extreme that they name: `cache_len`: some request holds exactly 4096 positions in every draw. `tree_parent`: node 0 is its own parent; every other node's parent is one of the three nodes before it. `valid_nodes`: the 1 entries of each request form a prefix of 32 to 64 nodes. `accepted_path`: each row is a chain in which every node is the parent of the next (node 0 may repeat at the start), ending at the request's last real node. `slot_owner`: each slot is named once.
All inputs are finite; a program needn't handle non-finite values.
Results may differ from a plain program's by a relative error of at most 0.007.
The roundings to bfloat16 on the way count: a program that leaves them out, or rounds other values in their place, can miss the bound.
Values may be sent and summed in bfloat16 or wider, within the bound.
No kernel may reach another device: no remote copies, remote signals or barrier semaphores. Data moves between devices by JAX's collectives and lax.ppermute only.
A program may use at most 128 MiB of HBM per device.

v0:
```python
import math
import jax
import jax.numpy as jnp
from jax import lax
from jax.sharding import PartitionSpec as P

GROUP = 7
epsilon = 1e-05
rope_base = 5000000.0
masked_score = -1e30


def from_partner(block, axis, stride):
    count = lax.axis_size(axis)
    route = []
    for low in range(count):
        high = low | 1 << stride
        if high != low and high < count:
            route += [(low, high), (high, low)]
    return lax.ppermute(block, axis, route)


def tree_closure(parents):
    width = parents.shape[-1]
    nodes = jnp.arange(width, dtype=jnp.int32)
    onehot = (parents[..., None] == nodes).astype(jnp.float32)
    reach = jnp.minimum(jnp.eye(width, dtype=jnp.float32) + onehot, 1.0)
    for rounds in range((width - 1).bit_length()):
        reach = jnp.minimum(
            jnp.einsum("rij,rjk->rik", reach, reach, precision=lax.Precision.HIGHEST), 1.0
        )
    return reach


def rotate(values, positions):
    head_dim = values.shape[-1]
    half_dim = head_dim // 2
    freq_steps = jnp.arange(half_dim, dtype=jnp.float32)
    inverse = jnp.exp(freq_steps * (-2.0 * math.log(rope_base) / head_dim))
    angles = positions[..., None] * inverse
    cosine = jnp.concatenate([jnp.cos(angles), jnp.cos(angles)], -1)[..., None, :]
    sine = jnp.concatenate([jnp.sin(angles), jnp.sin(angles)], -1)[..., None, :]
    turned = jnp.concatenate([-values[..., half_dim:], values[..., :half_dim]], -1)
    return values * cosine + turned * sine


def shards(
    hidden_in,
    norm_gain,
    w_query,
    w_key,
    w_value,
    w_out,
    key_cache,
    value_cache,
    cache_len,
    tree_parent,
    valid_nodes,
    accepted_path,
    slot_owner,
):
    req_dev, tree_size, part_width = hidden_in.shape
    row_count = req_dev * tree_size
    head_dim = key_cache.shape[-1]
    half_len = key_cache.shape[3]
    kv_group = key_cache.shape[2]
    q_cols = w_query.shape[1]
    k_cols = w_key.shape[1]
    gathered, full_gain = (
        lax.all_gather(hidden_in, "mp", axis=2, tiled=True),
        lax.all_gather(norm_gain, "mp", axis=0, tiled=True),
    )
    widened = gathered.astype(jnp.float32)
    meansq = jnp.mean(widened * widened, -1, keepdims=True)
    normed = (widened * lax.rsqrt(meansq + epsilon) * full_gain.astype(jnp.float32)).astype(
        jnp.bfloat16
    )
    flat = normed.reshape(row_count, gathered.shape[2])
    pieces = (
        lax.all_gather(w_query, "dp", axis=0, tiled=True),
        lax.all_gather(w_key, "dp", axis=0, tiled=True),
        lax.all_gather(w_value, "dp", axis=0, tiled=True),
    )
    query_sum, key_sum, value_sum = tuple(
        (jnp.dot(flat, piece, preferred_element_type=jnp.float32) for piece in pieces)
    )
    query = query_sum.astype(jnp.bfloat16)
    key_new = key_sum.astype(jnp.bfloat16)
    value_new = value_sum.astype(jnp.bfloat16)
    other_query, other_key, other_value = from_partner((query, key_new, value_new), "mp", 0)
    half_index = lax.axis_index("mp") % 2
    is_first = half_index == 0

    def paired(own_part, other_part):
        return jnp.where(
            is_first,
            jnp.concatenate([own_part, other_part], 1),
            jnp.concatenate([other_part, own_part], 1),
        )

    group_query = paired(query, other_query)
    group_key = paired(key_new, other_key)
    group_value = paired(value_new, other_value)
    reach = tree_closure(tree_parent)
    depth = jnp.sum(reach, -1) - 1.0
    position = cache_len[:, None].astype(jnp.float32) + depth
    rot_query = rotate(
        group_query.reshape(req_dev, tree_size, kv_group * GROUP, head_dim).astype(jnp.float32),
        position,
    ).astype(jnp.bfloat16)
    rot_key = rotate(
        group_key.reshape(req_dev, tree_size, kv_group, head_dim).astype(jnp.float32), position
    ).astype(jnp.bfloat16)
    node_values = group_value.reshape(req_dev, tree_size, kv_group, head_dim)
    queries_all = (
        rot_query.reshape(req_dev, tree_size, kv_group, GROUP, head_dim)
        .transpose(0, 2, 3, 1, 4)
        .reshape(req_dev, kv_group, GROUP * tree_size, head_dim)
    )
    scale = 1.0 / math.sqrt(head_dim)

    def one_request(packed):
        queries, key_r, value_r, cached_keys, cached_values, length, reach_r = packed
        tree_keys = key_r.transpose(1, 0, 2)
        tree_values = value_r.transpose(1, 0, 2)
        count = jnp.clip(length - half_index * half_len, 0, half_len)
        scores_tree = (
            jnp.einsum("gqd,gkd->gqk", queries, tree_keys, preferred_element_type=jnp.float32)
            * scale
        )
        tiled = jnp.logical_and(jnp.tile(reach_r, (GROUP, 1)) > 0.5, is_first)
        scores_tree = jnp.where(tiled[None], scores_tree, masked_score)
        scores_cache = (
            jnp.einsum("gqd,gkd->gqk", queries, cached_keys, preferred_element_type=jnp.float32)
            * scale
        )
        live = jnp.arange(half_len, dtype=jnp.int32) < count
        scores_cache = jnp.where(live[None, None, :], scores_cache, masked_score)
        highest = jnp.maximum(jnp.max(scores_cache, -1), jnp.max(scores_tree, -1))
        probs_cache = jnp.exp(scores_cache - highest[..., None]).astype(jnp.bfloat16)
        probs_tree = jnp.exp(scores_tree - highest[..., None]).astype(jnp.bfloat16)
        totals = jnp.sum(probs_cache.astype(jnp.float32), -1) + jnp.sum(
            probs_tree.astype(jnp.float32), -1
        )
        weighted = jnp.einsum(
            "gqk,gkd->gqd", probs_cache, cached_values, preferred_element_type=jnp.float32
        )
        weighted = weighted + jnp.einsum(
            "gqk,gkd->gqd", probs_tree, tree_values, preferred_element_type=jnp.float32
        )
        return (highest, totals, weighted)

    highest, totals, weighted = lax.map(
        one_request,
        (queries_all, rot_key, node_values, key_cache[:, 0], value_cache[:, 0], cache_len, reach),
    )
    other_high, other_totals, other_weighted = from_partner((highest, totals, weighted), "mp", 0)
    ceiling = jnp.maximum(highest, other_high)
    own_factor = jnp.exp(highest - ceiling)
    other_factor = jnp.exp(other_high - ceiling)
    numerator = weighted * own_factor[..., None] + other_weighted * other_factor[..., None]
    denominator = totals * own_factor + other_totals * other_factor
    attended = (numerator / denominator[..., None]).astype(jnp.bfloat16)
    attended = (
        attended.reshape(req_dev, kv_group, GROUP, tree_size, head_dim)
        .transpose(0, 3, 1, 2, 4)
        .reshape(req_dev, tree_size, kv_group * GROUP * head_dim)
    )
    attended = attended * valid_nodes[..., None].astype(jnp.bfloat16)
    own_heads = lax.dynamic_slice_in_dim(
        attended.reshape(row_count, 2 * q_cols), half_index * q_cols, q_cols, 1
    )
    terms = jnp.dot(
        own_heads,
        lax.all_gather(w_out, "dp", axis=1, tiled=True),
        preferred_element_type=jnp.float32,
    )
    mine = lax.psum_scatter(terms, "mp", scatter_dimension=1, tiled=True)
    layer_out = (
        (hidden_in.reshape(row_count, part_width).astype(jnp.float32) + mine)
        .astype(jnp.bfloat16)
        .reshape(req_dev, tree_size, part_width)
    )
    own_keys = lax.dynamic_slice_in_dim(
        rot_key.reshape(req_dev, tree_size, kv_group * head_dim), half_index * k_cols, k_cols, 2
    )
    kv_rows = jnp.stack([own_keys, value_new.reshape(req_dev, tree_size, k_cols)], 2)
    chosen = jax.vmap(lambda rows_of, picks: jnp.take(rows_of, picks, axis=0))(
        kv_rows, accepted_path
    )
    every_row = lax.all_gather(chosen, "dp", axis=0, tiled=True)
    total_reqs = slot_owner.shape[0]
    my_slots = lax.axis_index("dp") * req_dev + jnp.arange(req_dev, dtype=jnp.int32)
    matches = slot_owner[None, :] == my_slots[:, None]
    senders = jnp.sum(jnp.where(matches, jnp.arange(total_reqs, dtype=jnp.int32)[None, :], 0), 1)
    accepted_kv = jnp.take(every_row, senders, axis=0)
    return (layer_out, accepted_kv)


def solution(mesh):
    placed = (
        P("dp", None, "mp"),
        P("mp"),
        P("dp", "mp"),
        P("dp", "mp"),
        P("dp", "mp"),
        P("mp", "dp"),
        P("dp", "mp", None, None, None),
        P("dp", "mp", None, None, None),
        P("dp"),
        P("dp", None),
        P("dp", None),
        P("dp", None),
        P(),
    )
    return jax.shard_map(
        shards,
        mesh=mesh,
        in_specs=placed,
        out_specs=(P("dp", None, "mp"), P("dp", None, None, "mp")),
        check_vma=False,
    )
```

profile of v0, /device:TPU:2, one launch (start us, length us, event | category | flops | bytes accessed | tf_op | source)
XLA Modules:
  0.0 352.2 jit_solution(6628368691060993493)
XLA Ops:
  7.2 2.0 copy.134
  9.3 0.7 all-gather.8.cloned.1.call-update
  10.1 2.0 copy.158
  12.2 1.3 dynamic-slice.1
  14.1 0.9 dynamic-update-slice
  15.0 69.3 %all-reduce = bf16[7168]{0:T(1024)(128)(2,1)S(1)} all-reduce(bf16[7168]{0:T(1024)(128)(2,1)S(1)} %dynamic-update-slice), channel_id=1, replica_groups=mesh['dp'=16,'mp'=16] {'mp'}, use_global_device_ids=true, to_apply=%add | all-reduce | flops 7168 | bytes 28672
  84.3 26.0 %all-gather = bf16[16,448,64]{1,2,0:T(8,128)(2,1)S(1)} all-gather(bf16[1,448,64]{1,2,0:T(8,128)(2,1)} %bitcast.153), channel_id=1, replica_groups=mesh['dp'=16,'mp'=16] {'dp'}, dimensions={0}, use_global_device_ids=true | all-gather | bytes 974848 | tf_op jit(solution)/shard_map/all_gather | solution.py:81
  110.9 1.2 reshape.579
  114.0 24.1 %all-gather.1 = bf16[16,448,64]{1,2,0:T(8,128)(2,1)S(1)} all-gather(bf16[1,448,64]{1,2,0:T(8,128)(2,1)S(1)} %bitcast.154), channel_id=1, replica_groups=mesh['dp'=16,'mp'=16] {'dp'}, dimensions={0}, use_global_device_ids=true | all-gather | bytes 974848 | tf_op jit(solution)/shard_map/all_gather | solution.py:82
  138.6 1.2 reshape.581
  140.4 0.8 pad_maximum_fusion
  141.2 11.3 %copy.135 = bf16[4,64,7168]{2,1,0:T(8,128)(2,1)} copy(bf16[4,64,7168]{1,0,2:T(4,128)(2,1)} %all-gather.6.cloned.1.call-done) | data formatting | bytes 7340032 | tf_op jit(solution)/shard_map/all_gather | solution.py:70
  152.5 3.0 fusion.22
  155.7 1.0 fusion.24
  156.7 1.2 convolution_convert_fusion.2
  158.6 1.2 convolution_convert_fusion.1
  160.0 1.8 collective-permute-start.2
  162.5 7.2 %convolution_convert_fusion = bf16[256,448]{0,1:T(8,128)(2,1)S(1)} fusion(bf16[256,7168]{1,0:T(8,128)(2,1)} %bitcast.138, bf16[7168,448]{1,0:T(8,128)(2,1)} %all-gather.8.cloned.1.call-done), kind=kOutput, calls=%fused_computation.41 | convolution fusion | flops 1644281856 | bytes 10321920 | tf_op jit(solution)/shard_map/dot_general | solution.py:85
  170.8 0.7 fusion.38
  171.6 5.6 %collective-permute-done = bf16[256,448]{0,1:T(8,128)(2,1)S(1)} collective-permute-done((bf16[256,448]{0,1:T(8,128)(2,1)S(1)}, bf16[256,448]{0,1:T(8,128)(2,1)S(1)}, u32[]{:S(2)}, u32[]{:S(2)}) %collective-permute-start) | collective-permute-done | bytes 229408 | tf_op jit(solution)/shard_map/ppermute | solution.py:20
  179.3 42.3 %while.16 = (s32[]{:T(128)}, f32[4,1,448]{2,1,0:T(1,128)S(1)}, f32[4,1,448]{2,1,0:T(1,128)S(1)}, f32[4,1,448,128]{3,2,1,0:T(8,128)S(1)}, s32[4]{0:T(128)S(1)}, /...) while((s32[]{:T(128)}, f32[4,1,448]{2,1,0:T(1,128)S(1)}, ...), condition=%wide.region_7.8_spmd, body=%wide.region_2.7_spmd.sunk | while | flops 496694400 | bytes 28287568 | solution.py:153
  180.6 3.6 %fusion.79 = (f32[448]{0:T(512)S(1)}, f32[448,2048]{1,0:T(8,128)}) fusion(pred[2048]{0:T(1024)(128)(4,1)S(1)} %iota_compare_fusion.5, bf16[4,1,2048,128]{3,2,1,0:T(8,128)(2,1)} %get-tuple-element.394, s32[]{:T(128)} %get-tuple-element.371, bf16[4,1,448,128]{3,2,1,0:T(8,128)(2,1)S(1)} %get-tuple-element.393), kind=kOutput, calls=%fused_computation.5.clone.1 | convolution fusion | flops 237633088 | bytes 4313856 | tf_op jit(solution)/shard_map/while/body/eval_jaxpr/gqd,gkd->gqk/dot_general | solution.py:134
  184.8 1.1 fusion.81
  185.9 3.1 fusion.82
  189.1 0.8 convert_reduce_fusion.4
  191.2 3.6 %fusion.79 = (f32[448]{0:T(512)S(1)}, f32[448,2048]{1,0:T(8,128)}) fusion(pred[2048]{0:T(1024)(128)(4,1)S(1)} %iota_compare_fusion.5, bf16[4,1,2048,128]{3,2,1,0:T(8,128)(2,1)} %get-tuple-element.394, s32[]{:T(128)} %get-tuple-element.371, bf16[4,1,448,128]{3,2,1,0:T(8,128)(2,1)S(1)} %get-tuple-element.393), kind=kOutput, calls=%fused_computation.5.clone.1 | convolution fusion | flops 237633088 | bytes 4313856 | tf_op jit(solution)/shard_map/while/body/eval_jaxpr/gqd,gkd->gqk/dot_general | solution.py:134
  195.4 1.1 fusion.81
  196.5 3.1 fusion.82
  199.6 0.8 convert_reduce_fusion.4
  201.8 3.6 %fusion.79 = (f32[448]{0:T(512)S(1)}, f32[448,2048]{1,0:T(8,128)}) fusion(pred[2048]{0:T(1024)(128)(4,1)S(1)} %iota_compare_fusion.5, bf16[4,1,2048,128]{3,2,1,0:T(8,128)(2,1)} %get-tuple-element.394, s32[]{:T(128)} %get-tuple-element.371, bf16[4,1,448,128]{3,2,1,0:T(8,128)(2,1)S(1)} %get-tuple-element.393), kind=kOutput, calls=%fused_computation.5.clone.1 | convolution fusion | flops 237633088 | bytes 4313856 | tf_op jit(solution)/shard_map/while/body/eval_jaxpr/gqd,gkd->gqk/dot_general | solution.py:134
  205.9 1.1 fusion.81
  207.1 3.1 fusion.82
  210.2 0.8 convert_reduce_fusion.4
  212.3 3.6 %fusion.79 = (f32[448]{0:T(512)S(1)}, f32[448,2048]{1,0:T(8,128)}) fusion(pred[2048]{0:T(1024)(128)(4,1)S(1)} %iota_compare_fusion.5, bf16[4,1,2048,128]{3,2,1,0:T(8,128)(2,1)} %get-tuple-element.394, s32[]{:T(128)} %get-tuple-element.371, bf16[4,1,448,128]{3,2,1,0:T(8,128)(2,1)S(1)} %get-tuple-element.393), kind=kOutput, calls=%fused_computation.5.clone.1 | convolution fusion | flops 237633088 | bytes 4313856 | tf_op jit(solution)/shard_map/while/body/eval_jaxpr/gqd,gkd->gqk/dot_general | solution.py:134
  216.5 1.1 fusion.81
  217.6 3.1 fusion.82
  220.7 0.8 convert_reduce_fusion.4
  221.6 0.8 collective-permute-start.4
  222.5 1.3 collective-permute-start.3
  223.7 0.8 collective-permute-start.5
  224.6 18.7 %collective-permute-done.3 = f32[4,1,448]{2,1,0:T(1,128)S(1)} collective-permute-done((f32[4,1,448]{2,1,0:T(1,128)S(1)}, f32[4,1,448]{2,1,0:T(1,128)S(1)}, u32[]{:S(2)}, u32[]{:S(2)}) %collective-permute-start.3) | collective-permute-done | bytes 7200 | tf_op jit(solution)/shard_map/ppermute | solution.py:20
  243.5 0.9 divide_convert_fusion
  244.8 8.3 %fusion.30 = f32[256,7168]{0,1:T(8,128)} fusion(bf16[448,7168]{0,1:T(8,128)(2,1)} %all-gather.10.cloned.1.call-done, bf16[256,896]{1,0:T(8,128)(2,1)S(1)} %bitcast.145, s32[]{:T(128)S(6)} %select_n.115, bf16[256]{0:T(256)(128)(2,1)S(1)} %mul.204), kind=kOutput, calls=%fused_computation.63 | convolution fusion | flops 1644625920 | bytes 14025220 | tf_op jit(solution)/shard_map/dot_general | solution.py:173
  253.1 0.9 copy-done.3
  256.1 16.2 %all_gather.27 = bf16[64,8,2,64]{3,1,2,0:T(8,128)(2,1)S(1)} all-gather(bf16[4,8,2,64]{3,1,2,0:T(8,128)(2,1)S(1)} %copy_select_fusion), channel_id=1, replica_groups=mesh['dp'=16,'mp'=16] {'dp'}, dimensions={0}, use_global_device_ids=true | all-gather | bytes 139264 | tf_op jit(solution)/shard_map/all_gather | solution.py:191
  273.6 70.2 %reduce-scatter.2.cloned.1.call-done = f32[256,448]{0,1:T(8,128)} async-done(((f32[256,7168]{0,1:T(8,128)}), f32[256,448]{0,1:T(8,128)}) %reduce-scatter.2.cloned.1.call-update) | async-done | bytes 458768 | tf_op jit(solution)/shard_map/reduce_scatter | solution.py:178
  343.7 1.1 add_convert_fusion
  344.8 0.8 copy.160
  (165 shorter events, 17.1 us)
Async XLA Ops:
  7.2 134.1 %all-gather.6.cloned.1.call-start = ((), (), s32[]{:S(2)}) async-start(), calls=%async_computation.1 | async-start | bytes 7798784 | tf_op jit(solution)/shard_map/all_gather | solution.py:70
  9.3 102.9 %copy-start.9 = (s32[4,64]{1,0:T(4,128)S(1)}, s32[4,64]{1,0:T(4,128)}, u32[]{:S(2)}) copy-start(s32[4,64]{1,0:T(4,128)} %param.24) | copy-start | bytes 3076
  9.3 153.2 %all-gather.8.cloned.1.call-start = ((), (), s32[]{:S(2)}) async-start(), calls=%async_computation.2 | async-start | bytes 7798784 | tf_op jit(solution)/shard_map/all_gather | solution.py:80
  10.0 234.8 %all-gather.10.cloned.1.call-start = ((), (), s32[]{:S(2)}) async-start(), calls=%async_computation.3 | async-start | bytes 7798784 | tf_op jit(solution)/shard_map/all_gather | solution.py:175
  12.1 331.7 %reduce-scatter.2.cloned.1.call-start = ((), (), s32[]{:S(2)}) async-start(), calls=%async_computation.4 | async-start | bytes 7798784 | tf_op jit(solution)/shard_map/reduce_scatter | solution.py:178
  84.3 29.6 %copy-start.10 = (s32[4]{0:T(128)S(1)}, s32[4]{0:T(128)}, u32[]{:S(2)}) copy-start(s32[4]{0:T(128)} %param.23) | copy-start | bytes 52
  84.3 29.6 %copy-start.6 = (bf16[448,64]{0,1:T(8,128)(2,1)S(1)}, bf16[448,64]{0,1:T(8,128)(2,1)}, u32[]{:S(2)}) copy-start(bf16[448,64]{0,1:T(8,128)(2,1)} %param.19) | copy-start | bytes 172036
  152.5 3.1 copy-start.2
  156.7 1.8 copy-start.1
  158.0 4.0 %collective-permute-start.1 = (bf16[256,64]{0,1:T(8,128)(2,1)S(1)}, bf16[256,64]{0,1:T(8,128)(2,1)S(1)}, u32[]{:S(2)}, u32[]{:S(2)}) collective-permute-start(bf16[256,64]{0,1:T(8,128)(2,1)S(1)} %convolution_convert_fusion.2), channel_id=1, source_target_pairs={{0,1},{1,0},{2,3},{3,2},{4,5},{5,4},{6,7},{7,6},{8,9},{9,8},{10,11... | collective-permute-start | bytes 98312 | tf_op jit(solution)/shard_map/ppermute | solution.py:20
  160.0 10.7 %collective-permute-start.2 = (bf16[256,64]{0,1:T(8,128)(2,1)S(1)}, bf16[256,64]{0,1:T(8,128)(2,1)S(1)}, u32[]{:S(2)}, u32[]{:S(2)}) collective-permute-start(bf16[256,64]{0,1:T(8,128)(2,1)S(1)} %convolution_convert_fusion.1), channel_id=1, source_target_pairs={{0,1},{1,0},{2,3},{3,2},{4,5},{5,4},{6,7},{7,6},{8,9},{9,8},{10,11... | collective-permute-start | bytes 98312 | tf_op jit(solution)/shard_map/ppermute | solution.py:20
  169.7 7.4 %collective-permute-start = (bf16[256,448]{0,1:T(8,128)(2,1)S(1)}, bf16[256,448]{0,1:T(8,128)(2,1)S(1)}, u32[]{:S(2)}, u32[]{:S(2)}) collective-permute-start(bf16[256,448]{0,1:T(8,128)(2,1)S(1)} %convolution_convert_fusion), channel_id=1, source_target_pairs={{0,1},{1,0},{2,3},{3,2},{4,5},{5,4},{6,7},{7,6},{8,9},{9,8},{10,11... | collective-permute-start | bytes 688136 | tf_op jit(solution)/shard_map/ppermute | solution.py:20
  177.8 0.9 copy-start.5
  177.8 1.5 copy-start.4
  178.2 1.1 copy-start.11
  179.3 45.2 %copy-start.8 = (s32[4,64]{1,0:T(4,128)S(1)}, s32[4,64]{1,0:T(4,128)}, u32[]{:S(2)}) copy-start(s32[4,64]{1,0:T(4,128)} %param.25) | copy-start | bytes 3076
  184.5 4.5 %copy-start = (f32[448,2048]{1,0:T(8,128)S(1)}, f32[448,2048]{1,0:T(8,128)}, u32[]{:S(2)}) copy-start(f32[448,2048]{1,0:T(8,128)} %get-tuple-element.351) | copy-start | bytes 11010052 | tf_op jit(solution)/shard_map/while
  185.9 4.1 %copy-start.12 = (s32[4]{0:T(128)S(1)}, s32[4]{0:T(128)}, u32[]{:S(2)}) copy-start(s32[4]{0:T(128)} %get-tuple-element.447) | copy-start | bytes 52 | tf_op jit(solution)/shard_map/while
  195.2 4.5 %copy-start = (f32[448,2048]{1,0:T(8,128)S(1)}, f32[448,2048]{1,0:T(8,128)}, u32[]{:S(2)}) copy-start(f32[448,2048]{1,0:T(8,128)} %get-tuple-element.351) | copy-start | bytes 11010052 | tf_op jit(solution)/shard_map/while
  196.5 4.0 %copy-start.12 = (s32[4]{0:T(128)S(1)}, s32[4]{0:T(128)}, u32[]{:S(2)}) copy-start(s32[4]{0:T(128)} %get-tuple-element.447) | copy-start | bytes 52 | tf_op jit(solution)/shard_map/while
  205.7 4.5 %copy-start = (f32[448,2048]{1,0:T(8,128)S(1)}, f32[448,2048]{1,0:T(8,128)}, u32[]{:S(2)}) copy-start(f32[448,2048]{1,0:T(8,128)} %get-tuple-element.351) | copy-start | bytes 11010052 | tf_op jit(solution)/shard_map/while
  207.0 4.0 %copy-start.12 = (s32[4]{0:T(128)S(1)}, s32[4]{0:T(128)}, u32[]{:S(2)}) copy-start(s32[4]{0:T(128)} %get-tuple-element.447) | copy-start | bytes 52 | tf_op jit(solution)/shard_map/while
  216.3 4.5 %copy-start = (f32[448,2048]{1,0:T(8,128)S(1)}, f32[448,2048]{1,0:T(8,128)}, u32[]{:S(2)}) copy-start(f32[448,2048]{1,0:T(8,128)} %get-tuple-element.351) | copy-start | bytes 11010052 | tf_op jit(solution)/shard_map/while
  217.6 4.0 %copy-start.12 = (s32[4]{0:T(128)S(1)}, s32[4]{0:T(128)}, u32[]{:S(2)}) copy-start(s32[4]{0:T(128)} %get-tuple-element.447) | copy-start | bytes 52 | tf_op jit(solution)/shard_map/while
  221.6 21.8 %collective-permute-start.4 = (f32[4,1,448,128]{3,2,1,0:T(8,128)S(1)}, f32[4,1,448,128]{3,2,1,0:T(8,128)S(1)}, u32[]{:S(2)}, u32[]{:S(2)}) collective-permute-start(f32[4,1,448,128]{3,2,1,0:T(8,128)S(1)} %get-tuple-element.434), channel_id=1, source_target_pairs={{0,1},{1,0},{2,3},{3,2},{4,5},{5,4},{6,7},{7,6},{8,9},{9,8},{10,11... | collective-permute-start | bytes 2752520 | tf_op jit(solution)/shard_map/ppermute | solution.py:20
  222.5 20.8 %collective-permute-start.3 = (f32[4,1,448]{2,1,0:T(1,128)S(1)}, f32[4,1,448]{2,1,0:T(1,128)S(1)}, u32[]{:S(2)}, u32[]{:S(2)}) collective-permute-start(f32[4,1,448]{2,1,0:T(1,128)S(1)} %get-tuple-element.432), channel_id=1, source_target_pairs={{0,1},{1,0},{2,3},{3,2},{4,5},{5,4},{6,7},{7,6},{8,9},{9,8},{10,11... | collective-permute-start | bytes 21512 | tf_op jit(solution)/shard_map/ppermute | solution.py:20
  223.7 19.6 %collective-permute-start.5 = (f32[4,1,448]{2,1,0:T(1,128)S(1)}, f32[4,1,448]{2,1,0:T(1,128)S(1)}, u32[]{:S(2)}, u32[]{:S(2)}) collective-permute-start(f32[4,1,448]{2,1,0:T(1,128)S(1)} %get-tuple-element.433), channel_id=1, source_target_pairs={{0,1},{1,0},{2,3},{3,2},{4,5},{5,4},{6,7},{7,6},{8,9},{9,8},{10,11... | collective-permute-start | bytes 21512 | tf_op jit(solution)/shard_map/ppermute | solution.py:20
  253.1 0.9 copy-start.3
  253.1 1.2 copy-start.7
  253.1 1.3 copy-start.13
Sparse Core Ops, SparseCore 0:
  10.5 74.6 all-gather.5
  87.0 58.2 all-gather.7
  147.2 48.8 all-gather.9
  253.3 90.4 reduce-scatter.1
where the time goes:
time: 353 us; the launch traced here: 352 us
  blocking collectives  136 us (39%)
  waiting for transfers between devices  95.3 us (27%)
  matrix products  51.7 us (15%)
  local copies, waits for them, and re-layouts  31.7 us (9%)
  between operations  15 us (4%)
  other arithmetic  14.3 us (4%)
  starting transfers between devices  5.51 us (2%)
    reduce_scatter x1, waiting for transfers between devices, shards(): mine = lax.psum_scatter(terms, 'mp', scatter_dimension=1, tiled=True)  70.2 us
    unnamed x1, blocking collectives  69.3 us
    all_gather x1, blocking collectives, shards(): lax.all_gather(w_key, 'dp', axis=0, tiled=True)  26 us
    ppermute x6, waiting for transfers between devices, from_partner(): return lax.ppermute(block, axis, route)  24.4 us
    all_gather x1, blocking collectives, shards(): lax.all_gather(w_value, 'dp', axis=0, tiled=True)  24.1 us
    all_gather x1, blocking collectives, shards(): every_row = lax.all_gather(chosen, 'dp', axis=0, tiled=True)  16.2 us
    dot_general x4, matrix products, one_request(): jnp.einsum('gqd,gkd->gqk', queries, cached_keys, preferred_element_type=j...  14.5 us
    dot_general x4, matrix products, one_request(): jnp.einsum('gqk,gkd->gqd', probs_cache, cached_values, preferred_element_...  12.3 us
  transfers between devices with their start and end apart: 10, of which 4 were waited for; matrix products, arithmetic and copies ran while one was open for 24% of the time, Pallas kernels for 0%

commit v1 on v0

--- a/solution.py
+++ b/solution.py
@@ -8,6 +8,13 @@
 epsilon = 1e-05
 rope_base = 5000000.0
 masked_score = -1e30
+
+
+def advance_the_islands(local_array):
+    val2 = jnp.stack([local_array] * jax.lax.axis_size("mp"))
+    all_rows = jax.lax.all_to_all(val2, "mp", 0, 0)
+    e_next = jnp.concatenate(all_rows, axis=2)
+    return e_next
 
 
 def from_partner(block, axis, stride):
@@ -67,7 +74,7 @@
     q_cols = w_query.shape[1]
     k_cols = w_key.shape[1]
     gathered, full_gain = (
-        lax.all_gather(hidden_in, "mp", axis=2, tiled=True),
+        advance_the_islands(hidden_in),
         lax.all_gather(norm_gain, "mp", axis=0, tiled=True),
     )
     widened = gathered.astype(jnp.float32)

time: 353 us -> 409 us (1.16)
  blocking collectives: 136 us -> 175 us
  starting transfers between devices: 5.51 us -> 12.7 us
  other arithmetic: 14.3 us -> 20.9 us
  local copies, waits for them, and re-layouts: 31.7 us -> 37.2 us
    unnamed x1, blocking collectives: 69.3 us -> 118 us
    convert_element_type x0 -> x2, local copies, waits for them, and re-layouts: none -> 17.8 us  [shards(): widened = gathered.astype(jnp.float32)]
    all_gather x1 -> x0, local copies, waits for them, and re-layouts: 11.3 us -> none  [shards(): lax.all_gather(hidden_in, 'mp', axis=2, tiled=True)]
    all_to_all x0 -> x1, starting transfers between devices: none -> 7.62 us  [advance_the_islands(): all_rows = jax.lax.all_to_all(val2, 'mp', 0, 0)]
    all_gather x1, blocking collectives: 24.1 us -> 17.7 us  [shards(): lax.all_gather(w_value, 'dp', axis=0, tiled=True)]
    unnamed x36 -> x41, local copies, waits for them, and re-layouts: 11.3 us -> 6.74 us
  transfers between devices with their start and end apart: 10 -> 10, of which waited for: 4 -> 5; matrix products, arithmetic and copies ran while one was open for 24% -> 24% of each run, Pallas kernels for 0% -> 0%
where the time goes in v1:
time: 409 us; the launch traced here: 408 us
  blocking collectives  175 us (43%)
  waiting for transfers between devices  93.2 us (23%)
  matrix products  50.9 us (12%)
  local copies, waits for them, and re-layouts  37.2 us (9%)
  other arithmetic  20.9 us (5%)
  between operations  15 us (4%)
  starting transfers between devices  12.7 us (3%)
    unnamed x1, blocking collectives  118 us
    reduce_scatter x1, waiting for transfers between devices, shards(): mine = lax.psum_scatter(terms, 'mp', scatter_dimension=1, tiled=True)  68.2 us
    ppermute x6, waiting for transfers between devices, from_partner(): return lax.ppermute(block, axis, route)  24.2 us
    all_gather x1, blocking collectives, shards(): lax.all_gather(w_key, 'dp', axis=0, tiled=True)  22.9 us
    convert_element_type x2, local copies, waits for them, and re-layouts, shards(): widened = gathered.astype(jnp.float32)  17.8 us
    all_gather x1, blocking collectives, shards(): lax.all_gather(w_value, 'dp', axis=0, tiled=True)  17.7 us
    all_gather x1, blocking collectives, shards(): every_row = lax.all_gather(chosen, 'dp', axis=0, tiled=True)  16.5 us
    dot_general x4, matrix products, one_request(): jnp.einsum('gqd,gkd->gqk', queries, cached_keys, preferred_element_type=j...  14 us
  transfers between devices with their start and end apart: 10, of which 5 were waited for; matrix products, arithmetic and copies ran while one was open for 24% of the time, Pallas kernels for 0%

profile of v1, /device:TPU:2, one launch (start us, length us, event | category | flops | bytes accessed | tf_op | source)
XLA Modules:
  0.0 408.1 jit_solution(7343243048219357958)
XLA Ops:
  7.2 0.7 all-gather.5.cloned.1.call-update
  7.9 3.5 stack.4
  11.4 7.6 %all-to-all-start = ((bf16[16,4,64,448]{3,2,1,0:T(8,128)(2,1)}), bf16[16,4,64,448]{3,2,1,0:T(8,128)(2,1)}, u32[]{:S(2)}, u32[]{:S(2)}) async-start(bf16[16,4,64,448]{3,2,1,0:T(8,128)(2,1)} %stack.4), calls=%async_computation | async-start | bytes 8388608 | tf_op jit(solution)/shard_map/all_to_all | solution.py:15
  19.1 1.0 copy.127
  21.8 117.9 %all-reduce = bf16[7168]{0:T(1024)(128)(2,1)S(1)} all-reduce(bf16[7168]{0:T(1024)(128)(2,1)S(1)} %dynamic-update-slice), channel_id=1, replica_groups=mesh['dp'=16,'mp'=16] {'mp'}, use_global_device_ids=true, to_apply=%add | all-reduce | flops 7168 | bytes 28672
  139.7 22.9 %all-gather = bf16[16,448,64]{1,2,0:T(8,128)(2,1)S(1)} all-gather(bf16[1,448,64]{1,2,0:T(8,128)(2,1)S(1)} %bitcast.153), channel_id=1, replica_groups=mesh['dp'=16,'mp'=16] {'dp'}, dimensions={0}, use_global_device_ids=true | all-gather | bytes 974848 | tf_op jit(solution)/shard_map/all_gather | solution.py:88
  163.2 1.2 reshape.592
  164.4 17.7 %all-gather.1 = bf16[16,448,64]{1,2,0:T(8,128)(2,1)S(1)} all-gather(bf16[1,448,64]{1,2,0:T(8,128)(2,1)S(1)} %bitcast.154), channel_id=1, replica_groups=mesh['dp'=16,'mp'=16] {'dp'}, dimensions={0}, use_global_device_ids=true | all-gather | bytes 974848 | tf_op jit(solution)/shard_map/all_gather | solution.py:89
  182.7 1.2 reshape.594
  186.3 0.8 pad_maximum_fusion
  187.1 3.4 convert_bitcast_fusion
  190.5 8.1 %copy.104 = f32[4,64,16,448]{3,2,1,0:T(8,128)} copy(f32[4,64,16,448]{3,1,0,2:T(8,128)S(1)} %convert_bitcast_fusion) | data formatting | bytes 14680064 | tf_op jit(solution)/shard_map/convert_element_type | solution.py:80
  198.6 9.7 %reshape.566 = f32[256,7168]{1,0:T(8,128)} reshape(f32[4,64,16,448]{3,2,1,0:T(8,128)} %copy.104) | data formatting | bytes 14680064 | tf_op jit(solution)/shard_map/convert_element_type | solution.py:80
  208.3 3.2 fusion.22
  211.6 4.1 multiply_convert_fusion
  215.6 1.2 convolution_convert_fusion.2
  217.4 1.2 convolution_convert_fusion.1
  218.9 1.7 collective-permute-start.2
  221.4 7.0 %convolution_convert_fusion = bf16[256,448]{0,1:T(8,128)(2,1)S(1)} fusion(bf16[256,7168]{1,0:T(8,128)(2,1)} %copy-done.1, bf16[7168,448]{1,0:T(8,128)(2,1)} %all-gather.5.cloned.1.call-done), kind=kOutput, calls=%fused_computation.40 | convolution fusion | flops 1644281856 | bytes 10321920 | tf_op jit(solution)/shard_map/dot_general | solution.py:92
  229.2 0.7 fusion.36
  230.0 5.6 %collective-permute-done = bf16[256,448]{0,1:T(8,128)(2,1)S(1)} collective-permute-done((bf16[256,448]{0,1:T(8,128)(2,1)S(1)}, bf16[256,448]{0,1:T(8,128)(2,1)S(1)}, u32[]{:S(2)}, u32[]{:S(2)}) %collective-permute-start) | collective-permute-done | bytes 229408 | tf_op jit(solution)/shard_map/ppermute | solution.py:27
  237.7 42.0 %while.16 = (s32[]{:T(128)}, f32[4,1,448]{2,1,0:T(1,128)S(1)}, f32[4,1,448]{2,1,0:T(1,128)S(1)}, f32[4,1,448,128]{3,2,1,0:T(8,128)S(1)}, s32[4]{0:T(128)S(1)}, /...) while((s32[]{:T(128)}, f32[4,1,448]{2,1,0:T(1,128)S(1)}, ...), condition=%wide.region_7.8_spmd, body=%wide.region_2.7_spmd.sunk | while | flops 496694400 | bytes 28287568 | solution.py:160
  239.3 3.5 fusion.77
  243.3 1.1 fusion.79
  244.4 3.1 fusion.80
  247.6 0.8 convert_reduce_fusion.4
  249.7 3.5 fusion.77
  253.8 1.1 fusion.79
  254.9 3.1 fusion.80
  258.0 0.8 convert_reduce_fusion.4
  260.2 3.5 fusion.77
  264.2 1.1 fusion.79
  265.3 3.1 fusion.80
  268.5 0.8 convert_reduce_fusion.4
  270.6 3.5 fusion.77
  274.7 1.1 fusion.79
  275.8 3.1 fusion.80
  278.9 0.8 convert_reduce_fusion.4
  279.8 0.8 collective-permute-start.4
  280.6 1.3 collective-permute-start.3
  281.9 0.7 collective-permute-start.5
  282.7 18.3 %collective-permute-done.3 = f32[4,1,448]{2,1,0:T(1,128)S(1)} collective-permute-done((f32[4,1,448]{2,1,0:T(1,128)S(1)}, f32[4,1,448]{2,1,0:T(1,128)S(1)}, u32[]{:S(2)}, u32[]{:S(2)}) %collective-permute-start.3) | collective-permute-done | bytes 7200 | tf_op jit(solution)/shard_map/ppermute | solution.py:27
  301.2 0.9 divide_convert_fusion
  302.6 8.3 %fusion.28 = f32[256,7168]{0,1:T(8,128)} fusion(bf16[448,7168]{0,1:T(8,128)(2,1)} %all-gather.7.cloned.1.call-done, bf16[256,896]{1,0:T(8,128)(2,1)S(1)} %bitcast.145, s32[]{:T(128)S(6)} %select_n.115, bf16[256]{0:T(256)(128)(2,1)S(1)} %mul.208), kind=kOutput, calls=%fused_computation.62 | convolution fusion | flops 1644625920 | bytes 14025220 | tf_op jit(solution)/shard_map/dot_general | solution.py:180
  313.8 16.5 %all_gather.23 = bf16[64,8,2,64]{3,1,2,0:T(8,128)(2,1)S(1)} all-gather(bf16[4,8,2,64]{3,1,2,0:T(8,128)(2,1)S(1)} %copy_select_fusion), channel_id=1, replica_groups=mesh['dp'=16,'mp'=16] {'dp'}, dimensions={0}, use_global_device_ids=true | all-gather | bytes 139264 | tf_op jit(solution)/shard_map/all_gather | solution.py:198
  331.5 68.2 %reduce-scatter.2.cloned.1.call-done = f32[256,448]{0,1:T(8,128)} async-done(((f32[256,7168]{0,1:T(8,128)}), f32[256,448]{0,1:T(8,128)}) %reduce-scatter.2.cloned.1.call-update) | async-done | bytes 458768 | tf_op jit(solution)/shard_map/reduce_scatter | solution.py:185
  399.7 1.1 add_convert_fusion
  400.8 0.8 copy.129
  (173 shorter events, 18.6 us)
Async XLA Ops:
  7.2 214.2 %all-gather.5.cloned.1.call-start = ((), (), s32[]{:S(2)}) async-start(), calls=%async_computation.2 | async-start | bytes 7798784 | tf_op jit(solution)/shard_map/all_gather | solution.py:87
  11.4 7.7 %copy-start.5 = (bf16[448,448]{1,0:T(8,128)(2,1)S(1)}, bf16[448,448]{1,0:T(8,128)(2,1)}, u32[]{:S(2)}) copy-start(bf16[448,448]{1,0:T(8,128)(2,1)} %param.20) | copy-start | bytes 1204228
  11.4 8.8 %copy-start.16 = (u32[256]{0:T(256)S(1)}, u32[256]{0:T(256)}, u32[]{:S(2)}) copy-start(u32[256]{0:T(256)} %constant.151) | copy-start | bytes 3076
  11.4 10.1 %copy-start.11 = (bf16[448]{0:T(512)(128)(2,1)S(1)}, bf16[448]{0:T(512)(128)(2,1)}, u32[]{:S(2)}) copy-start(bf16[448]{0:T(512)(128)(2,1)} %param.16) | copy-start | bytes 2692
  11.4 128.3 %copy-start.6 = (bf16[448,64]{0,1:T(8,128)(2,1)S(1)}, bf16[448,64]{0,1:T(8,128)(2,1)}, u32[]{:S(2)}) copy-start(bf16[448,64]{0,1:T(8,128)(2,1)} %param.18) | copy-start | bytes 172036
  11.4 175.7 %all-to-all-start = ((bf16[16,4,64,448]{3,2,1,0:T(8,128)(2,1)}), bf16[16,4,64,448]{3,2,1,0:T(8,128)(2,1)}, u32[]{:S(2)}, u32[]{:S(2)}) async-start(bf16[16,4,64,448]{3,2,1,0:T(8,128)(2,1)} %stack.4), calls=%async_computation | async-start | bytes 8388608 | tf_op jit(solution)/shard_map/all_to_all | solution.py:15
  19.0 145.3 %copy-start.12 = (s32[4]{0:T(128)S(1)}, s32[4]{0:T(128)}, u32[]{:S(2)}) copy-start(s32[4]{0:T(128)} %param.23) | copy-start | bytes 52
  19.0 145.4 %copy-start.7 = (bf16[448,64]{0,1:T(8,128)(2,1)S(1)}, bf16[448,64]{0,1:T(8,128)(2,1)}, u32[]{:S(2)}) copy-start(bf16[448,64]{0,1:T(8,128)(2,1)} %param.19) | copy-start | bytes 172036
  19.1 283.5 %all-gather.7.cloned.1.call-start = ((), (), s32[]{:S(2)}) async-start(), calls=%async_computation.3 | async-start | bytes 7798784 | tf_op jit(solution)/shard_map/all_gather | solution.py:182
  20.1 379.6 %reduce-scatter.2.cloned.1.call-start = ((), (), s32[]{:S(2)}) async-start(), calls=%async_computation.4 | async-start | bytes 7798784 | tf_op jit(solution)/shard_map/reduce_scatter | solution.py:185
  163.2 20.7 %copy-start.10 = (s32[4,64]{1,0:T(4,128)S(1)}, s32[4,64]{1,0:T(4,128)}, u32[]{:S(2)}) copy-start(s32[4,64]{1,0:T(4,128)} %param.24) | copy-start | bytes 3076
  215.6 1.8 copy-start.1
  216.9 4.0 collective-permute-start.1
  218.9 10.2 %collective-permute-start.2 = (bf16[256,64]{0,1:T(8,128)(2,1)S(1)}, bf16[256,64]{0,1:T(8,128)(2,1)S(1)}, u32[]{:S(2)}, u32[]{:S(2)}) collective-permute-start(bf16[256,64]{0,1:T(8,128)(2,1)S(1)} %convolution_convert_fusion.1), channel_id=1, source_target_pairs={{0,1},{1,0},{2,3},{3,2},{4,5},{5,4},{6,7},{7,6},{8,9},{9,8},{10,11... | collective-permute-start | bytes 98312 | tf_op jit(solution)/shard_map/ppermute | solution.py:27
  228.4 7.2 %collective-permute-start = (bf16[256,448]{0,1:T(8,128)(2,1)S(1)}, bf16[256,448]{0,1:T(8,128)(2,1)S(1)}, u32[]{:S(2)}, u32[]{:S(2)}) collective-permute-start(bf16[256,448]{0,1:T(8,128)(2,1)S(1)} %convolution_convert_fusion), channel_id=1, source_target_pairs={{0,1},{1,0},{2,3},{3,2},{4,5},{5,4},{6,7},{7,6},{8,9},{9,8},{10,11... | collective-permute-start | bytes 688136 | tf_op jit(solution)/shard_map/ppermute | solution.py:27
  236.2 0.9 copy-start.4
  236.2 1.5 copy-start.3
  236.6 1.1 copy-start.13
  237.7 44.9 %copy-start.9 = (s32[4,64]{1,0:T(4,128)S(1)}, s32[4,64]{1,0:T(4,128)}, u32[]{:S(2)}) copy-start(s32[4,64]{1,0:T(4,128)} %param.25) | copy-start | bytes 3076
  243.1 4.5 %copy-start = (f32[448,2048]{1,0:T(8,128)S(1)}, f32[448,2048]{1,0:T(8,128)}, u32[]{:S(2)}) copy-start(f32[448,2048]{1,0:T(8,128)} %get-tuple-element.336) | copy-start | bytes 11010052 | tf_op jit(solution)/shard_map/while
  244.4 4.0 copy-start.14
  253.6 4.5 %copy-start = (f32[448,2048]{1,0:T(8,128)S(1)}, f32[448,2048]{1,0:T(8,128)}, u32[]{:S(2)}) copy-start(f32[448,2048]{1,0:T(8,128)} %get-tuple-element.336) | copy-start | bytes 11010052 | tf_op jit(solution)/shard_map/while
  254.9 4.0 copy-start.14
  264.0 4.5 %copy-start = (f32[448,2048]{1,0:T(8,128)S(1)}, f32[448,2048]{1,0:T(8,128)}, u32[]{:S(2)}) copy-start(f32[448,2048]{1,0:T(8,128)} %get-tuple-element.336) | copy-start | bytes 11010052 | tf_op jit(solution)/shard_map/while
  265.3 4.0 copy-start.14
  274.4 4.5 %copy-start = (f32[448,2048]{1,0:T(8,128)S(1)}, f32[448,2048]{1,0:T(8,128)}, u32[]{:S(2)}) copy-start(f32[448,2048]{1,0:T(8,128)} %get-tuple-element.336) | copy-start | bytes 11010052 | tf_op jit(solution)/shard_map/while
  275.8 4.0 copy-start.14
  279.8 21.4 %collective-permute-start.4 = (f32[4,1,448,128]{3,2,1,0:T(8,128)S(1)}, f32[4,1,448,128]{3,2,1,0:T(8,128)S(1)}, u32[]{:S(2)}, u32[]{:S(2)}) collective-permute-start(f32[4,1,448,128]{3,2,1,0:T(8,128)S(1)} %get-tuple-element.417), channel_id=1, source_target_pairs={{0,1},{1,0},{2,3},{3,2},{4,5},{5,4},{6,7},{7,6},{8,9},{9,8},{10,11... | collective-permute-start | bytes 2752520 | tf_op jit(solution)/shard_map/ppermute | solution.py:27
  280.6 20.5 %collective-permute-start.3 = (f32[4,1,448]{2,1,0:T(1,128)S(1)}, f32[4,1,448]{2,1,0:T(1,128)S(1)}, u32[]{:S(2)}, u32[]{:S(2)}) collective-permute-start(f32[4,1,448]{2,1,0:T(1,128)S(1)} %get-tuple-element.415), channel_id=1, source_target_pairs={{0,1},{1,0},{2,3},{3,2},{4,5},{5,4},{6,7},{7,6},{8,9},{9,8},{10,11... | collective-permute-start | bytes 21512 | tf_op jit(solution)/shard_map/ppermute | solution.py:27
  281.9 19.2 %collective-permute-start.5 = (f32[4,1,448]{2,1,0:T(1,128)S(1)}, f32[4,1,448]{2,1,0:T(1,128)S(1)}, u32[]{:S(2)}, u32[]{:S(2)}) collective-permute-start(f32[4,1,448]{2,1,0:T(1,128)S(1)} %get-tuple-element.416), channel_id=1, source_target_pairs={{0,1},{1,0},{2,3},{3,2},{4,5},{5,4},{6,7},{7,6},{8,9},{9,8},{10,11... | collective-permute-start | bytes 21512 | tf_op jit(solution)/shard_map/ppermute | solution.py:27
  310.8 0.7 copy-start.8
  310.8 1.0 copy-start.2
  310.8 1.2 copy-start.15
Sparse Core Ops, SparseCore 0:
  9.8 53.9 all-gather.4
  65.7 49.4 all-gather.6
  311.0 88.6 reduce-scatter.1
